TPU v7x, 32 devices: a whole 2x2x4 slice. The times are simulated.
32 devices in a mesh: groups: 1, dp: 8 (over z, y), fsdp: 4 (over x, core).
Axes of the slice: x: 2, y: 2, z: 4, core: 2. Of those that a mesh axis runs over, the one named last changes fastest.
Arguments:
- activations: bfloat16 [4096, 4096], P(('groups', 'dp', 'fsdp')), may hold values from -6 to 6
- gate_values: bfloat16 [4096, 14336], P(('groups', 'dp'), 'fsdp'), may hold values from -6 to 6
- up_values: bfloat16 [4096, 14336], P(('groups', 'dp'), 'fsdp'), may hold values from -6 to 6
- cotangent: bfloat16 [4096, 4096], P(('groups', 'dp', 'fsdp')), may hold values from -6 to 6
- down_weight: bfloat16 [14336, 4096], P('fsdp', 'dp'), may hold values from -0.09375 to 0.09375
- up_entry: bfloat16 [64, 4096], replicated, may hold values from -0.09375 to 0.09375
- up_exit: bfloat16 [64, 14336], P(None, 'fsdp'), may hold values from -0.046875 to 0.046875
- down_entry: bfloat16 [64, 14336], P(None, 'fsdp'), may hold values from -0.046875 to 0.046875
- down_exit: bfloat16 [64, 4096], replicated, may hold values from -0.09375 to 0.09375
- queries: bfloat16 [1024, 2, 4096], P('dp', None, 'fsdp'), may hold values from -0.0029296875 to 0.0029296875
- fisher: bfloat16 [2, 4096, 4096], P(None, 'fsdp', 'dp'), may hold values from -1 to 4.5, as said below
Outputs:
- scores: float32 [1024, 8], P(('dp', 'fsdp'), 'groups')
Inputs may be any that keep to these rules, and one draw needn't show every extreme that they name: `fisher`: each layer's matrix is symmetric, its diagonal positive and larger than the rest of its row.
All inputs are finite; a program needn't handle non-finite values.
Results may differ from a plain program's by a relative error of at most 0.0029.
Values may be sent and summed in bfloat16 or wider, within the bound.
A program may use at most 128 MiB of HBM per device.

v0:
```python
import jax
import jax.numpy as jnp
from jax import lax
from jax.sharding import PartitionSpec as P

LEN = 512


def local(
    activations,
    gate_values,
    up_values,
    cotangent,
    down_weight,
    up_entry,
    up_exit,
    down_entry,
    down_exit,
    queries,
    fisher,
):
    highest = lax.Precision.HIGHEST
    tok_rows = activations.shape[0]
    side = up_entry.shape[0]
    gathered = lax.all_gather(cotangent, "fsdp", axis=0, tiled=True)
    contract = (((1,), (1,)), ((), ()))
    full_weight = lax.all_gather(down_weight, "dp", axis=1, tiled=True)
    back_hidden = lax.dot_general(
        gathered, full_weight, contract, preferred_element_type=jnp.float32
    )
    soft = jax.nn.silu(gate_values.astype(jnp.float32))
    act_down = (soft * up_values.astype(jnp.float32)).astype(jnp.bfloat16)
    grad_up = (back_hidden * soft).astype(jnp.bfloat16)
    part_out = lax.dot_general(grad_up, up_exit, contract, preferred_element_type=jnp.float32)
    part_in = lax.dot_general(act_down, down_entry, contract, preferred_element_type=jnp.float32)
    partial_value = jnp.concatenate([part_out, part_in], axis=1)
    mine = lax.psum_scatter(partial_value, "fsdp", scatter_dimension=0, tiled=True)
    out_up = mine[:, :side]
    in_down = mine[:, side:]
    in_up = lax.dot_general(activations, up_entry, contract, preferred_element_type=jnp.float32)
    out_down = lax.dot_general(cotangent, down_exit, contract, preferred_element_type=jnp.float32)
    seq_here = gathered.shape[0] // LEN
    position = lax.axis_index("fsdp") * tok_rows + jnp.arange(tok_rows, dtype=jnp.int32)
    member = (position[:, None] // LEN == jnp.arange(seq_here, dtype=jnp.int32)[None, :]).astype(
        jnp.float32
    )
    grad_first = jnp.einsum("ts,ti,tj->sij", member, in_up, out_up, precision=highest).reshape(
        seq_here, side * side
    )
    grad_second = jnp.einsum("ts,ti,tj->sij", member, in_down, out_down, precision=highest).reshape(
        seq_here, side * side
    )
    partial_grads = jnp.stack([grad_first, grad_second], axis=1)
    summed = lax.psum(partial_grads, "fsdp")
    spread = lax.all_to_all(summed, "dp", split_axis=2, concat_axis=0, tiled=True)
    applied_part = jnp.einsum("lkj,slj->slk", fisher.astype(jnp.float32), spread, precision=highest)
    applied = lax.psum(applied_part, "dp")
    flat_queries = queries.astype(jnp.float32).reshape(queries.shape[0], -1)
    terms = jnp.dot(flat_queries, applied.reshape(applied.shape[0], -1).T, precision=highest)
    return lax.psum_scatter(terms, "fsdp", scatter_dimension=0, tiled=True)


def solution(mesh):
    placed = (
        P(("groups", "dp", "fsdp"), None),
        P(("groups", "dp"), "fsdp"),
        P(("groups", "dp"), "fsdp"),
        P(("groups", "dp", "fsdp"), None),
        P("fsdp", "dp"),
        P(),
        P(None, "fsdp"),
        P(None, "fsdp"),
        P(),
        P("dp", None, "fsdp"),
        P(None, "fsdp", "dp"),
    )
    return jax.shard_map(
        local, mesh=mesh, in_specs=placed, out_specs=P(("dp", "fsdp"), "groups"), check_vma=False
    )
```

profile of v0, /device:TPU:0, one launch (start us, length us, event | category | flops | bytes accessed | tf_op | source)
XLA Modules:
  0.0 841.7 jit_solution(9429257184180446198)
XLA Ops:
  6.5 0.7 all-gather.3.cloned.1.call-update
  8.1 4.6 fusion.3
  12.7 33.5 %all-gather.3.cloned.1.call-done = bf16[512,4096]{1,0:T(8,128)(2,1)} async-done(((bf16[128,4096]{1,0:T(8,128)(2,1)}), bf16[512,4096]{1,0:T(8,128)(2,1)}) %all-gather.3.cloned.1.call-update) | async-done | bytes 4194320 | tf_op jit(solution)/shard_map/all_gather | solution.py:25
  46.1 560.7 %all-gather.5.cloned.1.call-done = bf16[3584,4096]{1,0:T(8,128)(2,1)} async-done(((bf16[3584,512]{1,0:T(8,128)(2,1)}), bf16[3584,4096]{1,0:T(8,128)(2,1)}) %all-gather.5.cloned.1.call-update) | async-done | bytes 29360144 | tf_op jit(solution)/shard_map/all_gather | solution.py:27
  606.8 25.0 %fusion.11 = f32[512,64]{0,1:T(8,128)S(1)} fusion(bf16[64,3584]{1,0:T(8,128)(2,1)} %param.17, bf16[512,4096]{1,0:T(8,128)(2,1)} %all-gather.3.cloned.1.call-done, bf16[3584,4096]{1,0:T(8,128)(2,1)} %all-gather.5.cloned.1.call-done, bf16[512,3584]{1,0:T(8,128)(2,1)} %param.12), kind=kOutput, calls=%fused_computation.26 | convolution fusion | flops 15280111616 | bytes 37814272 | tf_op jit(solution)/shard_map/dot_general | solution.py:34
  632.6 1.5 fusion.12
  634.1 1.8 convolution_multiply_fusion
  636.0 16.7 %reduce-scatter.5.cloned.1.call-done = f32[128,128]{0,1:T(8,128)} async-done(((f32[512,128]{0,1:T(8,128)}), f32[128,128]{0,1:T(8,128)}) %reduce-scatter.5.cloned.1.call-update) | async-done | bytes 65552 | tf_op jit(solution)/shard_map/reduce_scatter | solution.py:37
  652.7 0.9 fusion.6
  653.7 0.9 fusion.5
  654.8 3.7 copy.16
  658.5 41.2 %psum.14 = f32[1,2,4096]{1,0,2:T(1,128)} all-reduce(f32[1,2,4096]{1,0,2:T(1,128)} %copy.16), channel_id=1, replica_groups=mesh['groups'=1,'dp'=8,'fsdp'=4] {'fsdp'}, use_global_device_ids=true, to_apply=%region_1.2 | all-reduce | flops 8192 | bytes 65536 | tf_op jit(solution)/shard_map/psum | solution.py:54
  700.2 20.4 %reduce = f32[4096,2]{1,0:T(8,128)} reduce(f32[4096,1,2]{2,1,0:T(1,128)} %bitcast.36, f32[]{:T(128)} %broadcast.48), dimensions={1}, to_apply=%bitcast.13.reduce_sub_computation | reduce | bytes 65540
  720.6 3.1 reshape.37
  723.7 12.4 %all_to_all.18 = f32[8,1,1024]{2,1,0:T(1,128)S(1)} all-to-all(f32[8,1,1024]{2,1,0:T(1,128)S(1)} %reshape.37), channel_id=1, replica_groups=mesh['groups'=1,'dp'=8,'fsdp'=4] {'dp'}, dimensions={0} | all-to-all | bytes 65536 | tf_op jit(solution)/shard_map/all_to_all | solution.py:55
  736.0 0.7 reduce.1
  736.8 4.8 reshape.38
  741.5 2.2 copy.19
  743.7 2.4 convolution_bitcast_fusion
  746.2 65.8 %all-reduce.2.cloned.1.call-done = f32[8,2,1024]{2,0,1:T(8,128)} async-done(((f32[8,2,1024]{2,0,1:T(8,128)}), f32[8,2,1024]{2,0,1:T(8,128)}) %all-reduce.2.cloned.1.call-update) | async-done | bytes 65552 | tf_op jit(solution)/shard_map/psum | solution.py:57
  812.0 1.3 convolution_bitcast_fusion.1
  813.3 0.7 copy.20
  814.1 19.7 %reduce-scatter.7.cloned.1.call-done = f32[32,8]{1,0:T(8,128)} async-done(((f32[128,8]{1,0:T(8,128)}), f32[32,8]{1,0:T(8,128)}) %reduce-scatter.7.cloned.1.call-update) | async-done | bytes 1040
  833.8 1.4 copy.21
  (23 shorter events, 2.4 us)
Async XLA Ops:
  6.5 737.2 %copy-start = (bf16[2,1024,512]{2,1,0:T(8,128)(2,1)S(1)}, bf16[2,1024,512]{2,1,0:T(8,128)(2,1)}, u32[]{:S(2)}) copy-start(bf16[2,1024,512]{2,1,0:T(8,128)(2,1)} %param.21) | copy-start | bytes 6291460
  6.5 1.5 copy-start.3
  6.5 39.6 %all-gather.3.cloned.1.call-start = ((), (), s32[]{:S(2)}) async-start(), calls=%async_computation.3 | async-start | bytes 5242880 | tf_op jit(solution)/shard_map/all_gather | solution.py:25
  7.3 599.5 %all-gather.5.cloned.1.call-start = ((), (), s32[]{:S(2)}) async-start(), calls=%async_computation.4 | async-start | bytes 33030144 | tf_op jit(solution)/shard_map/all_gather | solution.py:27
  8.0 644.7 %reduce-scatter.5.cloned.1.call-start = ((), (), s32[]{:S(2)}) async-start(), calls=%async_computation.5 | async-start | bytes 327680 | tf_op jit(solution)/shard_map/reduce_scatter | solution.py:37
  12.7 619.9 %copy-start.1 = (bf16[128,4096]{1,0:T(8,128)(2,1)S(1)}, bf16[128,4096]{1,0:T(8,128)(2,1)}, u32[]{:S(2)}) copy-start(bf16[128,4096]{1,0:T(8,128)(2,1)} %param.14) | copy-start | bytes 3145732
  632.5 179.4 %all-reduce.2.cloned.1.call-start = ((), (), s32[]{:S(2)}) async-start(), calls=%async_computation.6 | async-start | bytes 131072 | tf_op jit(solution)/shard_map/psum | solution.py:57
  720.6 91.4 %copy-start.2 = (bf16[128,2,1024]{2,1,0:T(2,128)(2,1)S(1)}, bf16[128,2,1024]{2,1,0:T(2,128)(2,1)}, u32[]{:S(2)}) copy-start(bf16[128,2,1024]{2,1,0:T(2,128)(2,1)} %param.20) | copy-start | bytes 1572868
  746.1 87.6 %reduce-scatter.7.cloned.1.call-start = ((), (), s32[]{:S(2)}) async-start(), calls=%async_computation.7 | async-start | bytes 81920
Sparse Core Ops, SparseCore 0:
  8.9 37.1 all-gather.2
  47.7 559.0 all-gather.4
  632.7 19.9 reduce-scatter.4
  746.2 65.6 all-reduce.1
  814.4 19.3 reduce-scatter.6
where the time goes:
time: 842 us
  waiting for transfers between devices  698 us (83%)
  blocking collectives  53.6 us (6%)
  matrix products  38.5 us (5%)
  other arithmetic  21.9 us (3%)
  local copies, waits for them, and re-layouts  16.5 us (2%)
  between operations  13.3 us (2%)
    all_gather x1, waiting for transfers between devices, local(): full_weight = lax.all_gather(down_weight, 'dp', axis=1, tiled=True)  561 us
    psum x1, waiting for transfers between devices, local(): applied = lax.psum(applied_part, 'dp')  65.8 us
    psum x1, blocking collectives, local(): summed = lax.psum(partial_grads, 'fsdp')  41.2 us
    all_gather x1, waiting for transfers between devices, local(): gathered = lax.all_gather(cotangent, 'fsdp', axis=0, tiled=True)  33.5 us
    dot_general x1, matrix products, local(): lax.dot_general(grad_up, up_exit, contract, preferred_element_type=jnp.fl...  25 us
    unnamed x6, waiting for transfers between devices  21.1 us
    unnamed x1, other arithmetic  20.4 us
  transfers between devices with their start and end apart: 5, of which 5 were waited for; matrix products, arithmetic and copies ran while one was open for 1% of the time, Pallas kernels for 0%

commit v1 on v0

v1 whole, which is shorter than its diff:
```python
import functools

import jax
import jax.numpy as jnp
from jax import lax
from jax.experimental import pallas as pl
from jax.experimental.pallas import tpu as pltpu
from jax.sharding import PartitionSpec as P

LEN = 512
PAIR = 2
MESH = pl.DeviceIdType.MESH
HIGHEST = lax.Precision.HIGHEST
NT = (((1,), (1,)), ((), ()))
TN = (((0,), (0,)), ((), ()))
F32 = jnp.float32
BF16 = jnp.bfloat16


def silu(v):
    return v / (1.0 + jnp.exp(-v))


def halves(v):
    high = v.astype(BF16)
    low = (v - high.astype(F32)).astype(BF16)
    return jnp.concatenate([high, low], axis=0)


def kernel(
    dims,
    act_hbm,
    gate_hbm,
    up_hbm,
    cot_hbm,
    w_hbm,
    up_entry,
    up_exit,
    down_entry,
    down_exit,
    q_hbm,
    fisher_hbm,
    out_ref,
    wbuf,
    gbuf,
    ubuf,
    cotbuf,
    cloc,
    aloc,
    fbuf,
    qbuf,
    pbuf,
    out_acc,
    in_acc,
    gpart,
    abuf,
    gs,
    apart,
    bbuf,
    cpart,
    cbuf,
    ws_sem,
    wr_sem,
    gs_sem,
    gr_sem,
    loc_sem,
    snd_sem,
    rcv_sem,
):
    DP, FS, Z, T, TR, H, DL, CH, NC, R, S, SL, NI, KS, QS = dims
    N = DP * FS
    LAY = PAIR * FS
    gi = lax.axis_index("groups")
    d = lax.axis_index("dp")
    f = lax.axis_index("fsdp")
    z = lax.div(d, PAIR)
    y = lax.rem(d, PAIR)
    me = d * FS + f
    lm = y * FS + f

    def dev(flat):
        return (gi, lax.div(flat, FS), lax.rem(flat, FS))

    def lay_dev(q):
        return (gi, z * PAIR + lax.div(q, FS), lax.rem(q, FS))

    def remote(src, dst, ssem, rsem, to):
        return pltpu.make_async_remote_copy(
            src_ref=src, dst_ref=dst, send_sem=ssem, recv_sem=rsem, device_id=to, device_id_type=MESH
        )

    my_tok = pl.ds(pl.multiple_of(y * T, T), T)
    my_rows = pl.ds(pl.multiple_of(lm * TR, TR), TR)
    loads = [
        pltpu.make_async_copy(act_hbm, aloc, loc_sem.at[0]),
        pltpu.make_async_copy(cot_hbm, cloc, loc_sem.at[1]),
        pltpu.make_async_copy(gate_hbm, gbuf.at[my_tok, :], loc_sem.at[2]),
        pltpu.make_async_copy(up_hbm, ubuf, loc_sem.at[3]),
        pltpu.make_async_copy(w_hbm, wbuf.at[:, pl.ds(pl.multiple_of(z * DL, DL), DL)], loc_sem.at[4]),
        pltpu.make_async_copy(fisher_hbm, fbuf, loc_sem.at[5]),
    ]
    for load in loads:
        load.start()

    barrier = pltpu.get_barrier_semaphore()

    def greet(k, _):
        pl.semaphore_signal(barrier, inc=1, device_id=dev(lax.rem(me + k, N)), device_id_type=MESH)
        return 0

    lax.fori_loop(1, N, greet, 0)
    pl.semaphore_wait(barrier, N - 1)

    def wcopy(own, zz, c, way):
        rows = pl.ds(pl.multiple_of(c * CH, CH), CH)
        cols = pl.ds(pl.multiple_of(zz * DL, DL), DL)
        to = (z + 1 if way else z - 1) * PAIR + y
        src = w_hbm.at[rows, :] if own else wbuf.at[rows, cols]
        return remote(src, wbuf.at[rows, cols], ws_sem.at[way, zz, c], wr_sem.at[zz, c], (gi, to, f))

    def gcopy(c):
        cols = pl.ds(pl.multiple_of(c * CH, CH), CH)
        return remote(
            gate_hbm.at[:, cols],
            gbuf.at[my_tok, cols],
            gs_sem.at[c],
            gr_sem.at[c],
            (gi, z * PAIR + (1 - y), f),
        )

    def own_sends(c, _):
        @pl.when(z > 0)
        def _():
            wcopy(True, z, c, 0).start()

        @pl.when(z < Z - 1)
        def _():
            wcopy(True, z, c, 1).start()

        return 0

    lax.fori_loop(0, NC, own_sends, 0)

    def cot_piece(py, zz):
        return cot_hbm.at[:, pl.ds(pl.multiple_of((zz * PAIR + py) * DL, DL), DL)]

    for zz in range(Z):
        pltpu.make_async_copy(cot_piece(y, zz), cotbuf.at[my_rows, pl.ds(zz * DL, DL)], rcv_sem.at[0]).start()

    def cot_sends(k, _):
        q = lax.rem(lm + k, LAY)
        for zz in range(Z):
            remote(
                cot_piece(lax.div(q, FS), zz),
                cotbuf.at[my_rows, pl.ds(zz * DL, DL)],
                snd_sem.at[0],
                rcv_sem.at[0],
                lay_dev(q),
            ).start()
        return 0

    lax.fori_loop(1, LAY, cot_sends, 0)

    def gate_sends(c, _):
        gcopy(c).start()
        return 0

    lax.fori_loop(0, NC, gate_sends, 0)

    pltpu.make_async_copy(q_hbm.at[d], qbuf.at[d], rcv_sem.at[2]).start()

    def q_sends(k, _):
        to = lax.rem(d + k, DP)
        remote(q_hbm.at[to], qbuf.at[d], snd_sem.at[2], rcv_sem.at[2], (gi, to, f)).start()
        return 0

    lax.fori_loop(1, DP, q_sends, 0)

    loads[0].wait()
    loads[1].wait()
    pbuf[my_rows, 0:R] = lax.dot_general(aloc[...], up_entry[...], NT, preferred_element_type=F32)
    pbuf[my_rows, R : 2 * R] = lax.dot_general(cloc[...], down_exit[...], NT, preferred_element_type=F32)

    def p_sends(k, _):
        remote(
            pbuf.at[my_rows, :], pbuf.at[my_rows, :], snd_sem.at[1], rcv_sem.at[1], lay_dev(lax.rem(lm + k, LAY))
        ).start()
        return 0

    lax.fori_loop(1, LAY, p_sends, 0)

    TT = 256
    loads[2].wait()
    loads[3].wait()
    in_acc[...] = jnp.zeros_like(in_acc)
    out_acc[...] = jnp.zeros_like(out_acc)

    def down_chunk(c, _):
        cols = pl.ds(pl.multiple_of(c * CH, CH), CH)

        def down_tile(t, _):
            rows = pl.ds(pl.multiple_of(t * TT, TT), TT)
            grow = pl.ds(pl.multiple_of(y * T + t * TT, TT), TT)
            soft = silu(gbuf[grow, cols].astype(F32))
            hidden = (soft * ubuf[rows, cols].astype(F32)).astype(BF16)
            in_acc[rows, :] += lax.dot_general(hidden, down_entry[:, cols], NT, preferred_element_type=F32)
            return 0

        lax.fori_loop(0, T // TT, down_tile, 0)
        return 0

    lax.fori_loop(0, NC, down_chunk, 0)

    p_rest = pbuf.at[pl.ds(0, (LAY - 1) * TR), :]
    pltpu.make_async_copy(p_rest, p_rest, rcv_sem.at[1]).wait()
    for s in range(SL):
        rows = pl.ds(pl.multiple_of(y * T + s * LEN, LEN), LEN)
        g = lax.dot_general(
            in_acc[s * LEN : (s + 1) * LEN, :],
            pbuf[rows, R : 2 * R],
            TN,
            precision=HIGHEST,
            preferred_element_type=F32,
        )
        for dd in range(DP):
            gpart[dd, PAIR * SL + s] = g[dd * NI : (dd + 1) * NI, :]

    pltpu.make_async_copy(cotbuf, cotbuf, rcv_sem.at[0]).wait()
    loads[4].wait()

    def main_chunk(c, _):
        for k in range(1, Z):
            above = z + k
            below = z - k

            @pl.when(above < Z)
            def _():
                wcopy(False, above, c, 0).wait_recv()

            @pl.when((above < Z) & (z > 0))
            def _():
                wcopy(False, above, c, 0).start()

            @pl.when(below >= 0)
            def _():
                wcopy(False, below, c, 1).wait_recv()

            @pl.when((below >= 0) & (z < Z - 1))
            def _():
                wcopy(False, below, c, 1).start()

        cols = pl.ds(pl.multiple_of(c * CH, CH), CH)
        other = pl.ds(pl.multiple_of((1 - y) * T, T), T)
        remote(
            gate_hbm.at[:, cols], gbuf.at[other, cols], gs_sem.at[c], gr_sem.at[c], (gi, z * PAIR + (1 - y), f)
        ).wait_recv()

        def tile(t, _):
            rows = pl.ds(pl.multiple_of(t * TT, TT), TT)
            back = lax.dot_general(cotbuf[rows, :], wbuf[cols, :], NT, preferred_element_type=F32)
            grad = (back * silu(gbuf[rows, cols].astype(F32))).astype(BF16)
            out_acc[rows, :] += lax.dot_general(grad, up_exit[:, cols], NT, preferred_element_type=F32)
            return 0

        lax.fori_loop(0, PAIR * T // TT, tile, 0)
        return 0

    lax.fori_loop(0, NC, main_chunk, 0)

    for s in range(PAIR * SL):
        rows = slice(s * LEN, (s + 1) * LEN)
        g = lax.dot_general(pbuf[rows, 0:R], out_acc[rows, :], TN, precision=HIGHEST, preferred_element_type=F32)
        for dd in range(DP):
            gpart[dd, s] = g[dd * NI : (dd + 1) * NI, :]

    pltpu.make_async_copy(gpart.at[d], abuf.at[me], rcv_sem.at[3]).start()

    def a_sends(k, _):
        to = lax.rem(me + k, N)
        remote(gpart.at[lax.div(to, FS)], abuf.at[me], snd_sem.at[3], rcv_sem.at[3], dev(to)).start()
        return 0

    lax.fori_loop(1, N, a_sends, 0)
    loads[5].wait()
    pltpu.make_async_copy(abuf, abuf, rcv_sem.at[3]).wait()
    for zz in range(Z):
        total = abuf[zz * LAY, 0 : PAIR * SL]
        for m in range(1, LAY):
            total = total + abuf[zz * LAY + m, 0 : PAIR * SL]
        gs[0, zz * PAIR * SL : (zz + 1) * PAIR * SL] = total
    for dd in range(DP):
        total = abuf[dd * FS, PAIR * SL :]
        for m in range(1, FS):
            total = total + abuf[dd * FS + m, PAIR * SL :]
        gs[1, dd * SL : (dd + 1) * SL] = total
    for l in range(2):
        flat = jnp.concatenate([gs[l, :, i, :] for i in range(NI)], axis=1)
        both = lax.dot_general(halves(flat), fbuf[l], NT, preferred_element_type=F32)
        part = both[:S] + both[S:]
        for dd in range(DP):
            apart[dd, l * S : (l + 1) * S, :] = part[:, dd * KS : (dd + 1) * KS]

    pltpu.make_async_copy(apart.at[d], bbuf.at[d], rcv_sem.at[4]).start()

    def b_sends(k, _):
        to = lax.rem(d + k, DP)
        remote(apart.at[to], bbuf.at[d], snd_sem.at[4], rcv_sem.at[4], (gi, to, f)).start()
        return 0

    lax.fori_loop(1, DP, b_sends, 0)
    pltpu.make_async_copy(qbuf, qbuf, rcv_sem.at[2]).wait()
    pltpu.make_async_copy(bbuf, bbuf, rcv_sem.at[4]).wait()
    applied = bbuf[0]
    for dd in range(1, DP):
        applied = applied + bbuf[dd]
    wide = halves(jnp.concatenate([applied[:S], applied[S:]], axis=1))
    per = qbuf.shape[1]
    for dd in range(DP):
        both = lax.dot_general(wide, qbuf[dd], NT, preferred_element_type=F32)
        part = both[:S] + both[S:]
        for ff in range(FS):
            cpart[dd * FS + ff] = part[:, ff * QS : (ff + 1) * QS]

    pltpu.make_async_copy(cpart.at[me], cbuf.at[me], rcv_sem.at[5]).start()

    def c_sends(k, _):
        to = lax.rem(me + k, N)
        remote(cpart.at[to], cbuf.at[me], snd_sem.at[5], rcv_sem.at[5], dev(to)).start()
        return 0

    lax.fori_loop(1, N, c_sends, 0)

    def drain(ref, sem):
        pltpu.make_async_copy(ref, ref, sem).wait()

    for zz in range(Z):

        def chunk(c, _, zz=zz):
            @pl.when((z > 0) & (zz >= z))
            def _():
                wcopy(False, zz, c, 0).wait_send()

            @pl.when((z < Z - 1) & (zz <= z))
            def _():
                wcopy(False, zz, c, 1).wait_send()

            return 0

        lax.fori_loop(0, NC, chunk, 0)

    def gdrain(c, _):
        gcopy(c).wait_send()
        return 0

    lax.fori_loop(0, NC, gdrain, 0)
    drain(cotbuf.at[pl.ds(0, (LAY - 1) * TR), :], snd_sem.at[0])
    drain(p_rest, snd_sem.at[1])
    drain(qbuf.at[pl.ds(0, DP - 1)], snd_sem.at[2])
    drain(abuf.at[pl.ds(0, N - 1)], snd_sem.at[3])
    drain(bbuf.at[pl.ds(0, DP - 1)], snd_sem.at[4])
    drain(cbuf.at[pl.ds(0, N - 1)], snd_sem.at[5])

    drain(cbuf, rcv_sem.at[5])
    out_ref[...] = jnp.sum(cbuf[...], axis=0)


def local(
    shape,
    activations,
    gate_values,
    up_values,
    cotangent,
    down_weight,
    up_entry,
    up_exit,
    down_entry,
    down_exit,
    queries,
    fisher,
):
    DP, FS = shape
    Z = DP // PAIR
    T, H = gate_values.shape
    TR, D = cotangent.shape
    DL = down_weight.shape[1]
    R = up_entry.shape[0]
    CH = 256
    NC = H // CH
    SL = T // LEN
    S = DP * SL
    NI = fisher.shape[2] // R
    nq, _, kl = queries.shape
    KS = kl // DP
    N = DP * FS
    QS = nq // FS
    dims = (DP, FS, Z, T, TR, H, DL, CH, NC, R, S, SL, NI, KS, QS)
    moved = queries.reshape(nq, 2, DP, KS).transpose(2, 0, 1, 3).reshape(DP, nq, 2 * KS)
    hbm = pl.BlockSpec(memory_space=pl.ANY)
    vmem = pl.BlockSpec(memory_space=pltpu.VMEM)
    dma = pltpu.SemaphoreType.DMA
    out = pl.pallas_call(
        functools.partial(kernel, dims),
        out_shape=jax.ShapeDtypeStruct((S, QS), F32),
        in_specs=[hbm] * 5 + [vmem] * 4 + [hbm] * 2,
        out_specs=vmem,
        scratch_shapes=[
            pltpu.VMEM((H, Z * DL), BF16),
            pltpu.VMEM((PAIR * T, H), BF16),
            pltpu.VMEM((T, H), BF16),
            pltpu.VMEM((PAIR * T, Z * DL), BF16),
            pltpu.VMEM((TR, D), BF16),
            pltpu.VMEM((TR, D), BF16),
            pltpu.VMEM(fisher.shape, BF16),
            pltpu.VMEM((DP, nq, 2 * KS), BF16),
            pltpu.VMEM((PAIR * T, 2 * R), F32),
            pltpu.VMEM((PAIR * T, R), F32),
            pltpu.VMEM((T, R), F32),
            pltpu.VMEM((DP, (PAIR + 1) * SL, NI, R), F32),
            pltpu.VMEM((N, (PAIR + 1) * SL, NI, R), F32),
            pltpu.VMEM((2, S, NI, R), F32),
            pltpu.VMEM((DP, 2 * S, KS), F32),
            pltpu.VMEM((DP, 2 * S, KS), F32),
            pltpu.VMEM((N, S, QS), F32),
            pltpu.VMEM((N, S, QS), F32),
            dma((2, Z, NC)),
            dma((Z, NC)),
            dma((NC,)),
            dma((NC,)),
            dma((6,)),
            dma((6,)),
            dma((6,)),
        ],
        compiler_params=pltpu.CompilerParams(
            collective_id=0, has_side_effects=True, vmem_limit_bytes=58 * 1024 * 1024
        ),
    )(
        activations,
        gate_values,
        up_values,
        cotangent,
        down_weight,
        up_entry,
        up_exit,
        down_entry,
        down_exit,
        moved,
        fisher,
    )
    return out.T


def solution(mesh):
    placed = (
        P(("groups", "dp", "fsdp"), None),
        P(("groups", "dp"), "fsdp"),
        P(("groups", "dp"), "fsdp"),
        P(("groups", "dp", "fsdp"), None),
        P("fsdp", "dp"),
        P(),
        P(None, "fsdp"),
        P(None, "fsdp"),
        P(),
        P("dp", None, "fsdp"),
        P(None, "fsdp", "dp"),
    )
    return jax.shard_map(
        functools.partial(local, (mesh.shape["dp"], mesh.shape["fsdp"])),
        mesh=mesh,
        in_specs=placed,
        out_specs=P(("dp", "fsdp"), "groups"),
        check_vma=False,
    )
```

time: 842 us -> 335 us (0.40)
  waiting for transfers between devices: 698 us -> 0 us
  Pallas kernels: 0 us -> 331 us
  blocking collectives: 53.6 us -> 0 us
  matrix products: 38.5 us -> 0 us
  other arithmetic: 21.9 us -> 0 us
  between operations: 13.3 us -> 0.01 us
  local copies, waits for them, and re-layouts: 16.5 us -> 3.79 us
    all_gather x2 -> x0, waiting for transfers between devices: 594 us -> none  [the longest x1 561 us: local(): full_weight = lax.all_gather(down_weight, 'dp', axis=1, tiled=True)]
    pallas_call x0 -> x1, Pallas kernels: none -> 331 us  [local(): pl.pallas_call(functools.partial(kernel, dims), out_shape=jax.ShapeDtypeS...]
    psum x1 -> x0, waiting for transfers between devices: 65.8 us -> none  [local(): applied = lax.psum(applied_part, 'dp')]
    psum x1 -> x0, blocking collectives: 41.2 us -> none  [local(): summed = lax.psum(partial_grads, 'fsdp')]
    dot_general x8 -> x0, matrix products: 38.5 us -> none  [the longest x1 25 us: local(): lax.dot_general(grad_up, up_exit, contract, preferred_element_type=jnp.fl...]
    unnamed x6 -> x0, waiting for transfers between devices: 21.1 us -> none
    unnamed x1 -> x0, other arithmetic: 20.4 us -> none
    reduce_scatter x1 -> x0, waiting for transfers between devices: 16.7 us -> none  [local(): lax.psum_scatter(partial_value, 'fsdp', scatter_dimension=0, tiled=True)]
  transfers between devices with their start and end apart: 5 -> 0, of which waited for: 5 -> 0; matrix products, arithmetic and copies ran while one was open for 1% -> 0% of each run, Pallas kernels for 0% -> 0%
where the time goes in v1:
time: 335 us
  Pallas kernels  331 us (99%)
  local copies, waits for them, and re-layouts  3.79 us (1%)
    pallas_call x1, Pallas kernels, local(): pl.pallas_call(functools.partial(kernel, dims), out_shape=jax.ShapeDtypeS...  331 us

profile of v1, /device:TPU:0, one launch (start us, length us, event | category | flops | bytes accessed | tf_op | source)
XLA Modules:
  0.0 335.0 jit_solution(9133548407633191465)
XLA Ops:
  0.0 0.0 copy-start
  0.0 1.0 copy-done
  1.0 0.4 bitcast_bitcast_fusion
  1.4 1.1 reshape.7.q_hbm
  2.5 331.2 %shard_map.109 = f32[8,32]{1,0:T(8,128)} custom-call(bf16[128,4096]{1,0:T(8,128)(2,1)} %act_hbm.1, bf16[512,3584]{1,0:T(8,128)(2,1)} %gate_hbm.1, bf16[512,3584]{1,0:T(8,128)(2,1)} %up_hbm.1, bf16[128,4096]{1,0:T(8,128)(2,1)} %cot_hbm.1, bf16[3584,512]{1,0:T(8,128)(2,1)} %w_hbm.1, bf16[64,4096]{1,0:T(8,128)(2,1)} %up_entry.1, bf16[64,3584]{1,0:T(8,128)(2,1)} %up_exit.1, ...), custom_call_target="tpu_custom_call" | custom-call | tf_op jit(solution)/shard_map/pallas_call | solution.py:401
  333.8 1.3 copy.16
Async XLA Ops:
  0.0 1.0 copy-start

commit v2 on v1

--- a/solution.py
+++ b/solution.py
@@ -139,7 +139,6 @@
 
         return 0
 
-    lax.fori_loop(0, NC, own_sends, 0)
 
     def cot_piece(py, zz):
         return cot_hbm.at[:, pl.ds(pl.multiple_of((zz * PAIR + py) * DL, DL), DL)]
@@ -161,11 +160,7 @@
 
     lax.fori_loop(1, LAY, cot_sends, 0)
 
-    def gate_sends(c, _):
-        gcopy(c).start()
-        return 0
-
-    lax.fori_loop(0, NC, gate_sends, 0)
+    lax.fori_loop(0, NC, own_sends, 0)
 
     pltpu.make_async_copy(q_hbm.at[d], qbuf.at[d], rcv_sem.at[2]).start()
 
@@ -228,6 +223,10 @@
     pltpu.make_async_copy(cotbuf, cotbuf, rcv_sem.at[0]).wait()
     loads[4].wait()
 
+    gcopy(0).start()
+    gcopy(1).start()
+    gcopy(2).start()
+
     def main_chunk(c, _):
         for k in range(1, Z):
             above = z + k
@@ -250,6 +249,10 @@
                 wcopy(False, below, c, 1).start()
 
         cols = pl.ds(pl.multiple_of(c * CH, CH), CH)
+        @pl.when(c + 3 < NC)
+        def _():
+            gcopy(c + 3).start()
+
         other = pl.ds(pl.multiple_of((1 - y) * T, T), T)
         remote(
             gate_hbm.at[:, cols], gbuf.at[other, cols], gs_sem.at[c], gr_sem.at[c], (gi, z * PAIR + (1 - y), f)

time: 335 us -> 288 us (0.86)
  Pallas kernels: 331 us -> 284 us
    pallas_call x1, Pallas kernels: 331 us -> 284 us  [local(): pl.pallas_call(functools.partial(kernel, dims), out_shape=jax.ShapeDtypeS...]
where the time goes in v2:
time: 288 us
  Pallas kernels  284 us (99%)
  local copies, waits for them, and re-layouts  3.79 us (1%)
    pallas_call x1, Pallas kernels, local(): pl.pallas_call(functools.partial(kernel, dims), out_shape=jax.ShapeDtypeS...  284 us

profile of v2, /device:TPU:0, one launch (start us, length us, event | category | flops | bytes accessed | tf_op | source)
XLA Modules:
  0.0 288.1 jit_solution(773798360309855777)
XLA Ops:
  0.0 0.0 copy-start
  0.0 1.0 copy-done
  1.0 0.4 bitcast_bitcast_fusion
  1.4 1.1 reshape.7.q_hbm
  2.5 284.3 %shard_map.109 = f32[8,32]{1,0:T(8,128)} custom-call(bf16[128,4096]{1,0:T(8,128)(2,1)} %act_hbm.1, bf16[512,3584]{1,0:T(8,128)(2,1)} %gate_hbm.1, bf16[512,3584]{1,0:T(8,128)(2,1)} %up_hbm.1, bf16[128,4096]{1,0:T(8,128)(2,1)} %cot_hbm.1, bf16[3584,512]{1,0:T(8,128)(2,1)} %w_hbm.1, bf16[64,4096]{1,0:T(8,128)(2,1)} %up_entry.1, bf16[64,3584]{1,0:T(8,128)(2,1)} %up_exit.1, ...), custom_call_target="tpu_custom_call" | custom-call | tf_op jit(solution)/shard_map/pallas_call | solution.py:404
  286.8 1.3 copy.16
Async XLA Ops:
  0.0 1.0 copy-start

commit v3 on v2

--- a/solution.py
+++ b/solution.py
@@ -140,6 +140,9 @@
         return 0
 
 
+    FIRST = min(4, NC)
+    lax.fori_loop(0, FIRST, own_sends, 0)
+
     def cot_piece(py, zz):
         return cot_hbm.at[:, pl.ds(pl.multiple_of((zz * PAIR + py) * DL, DL), DL)]
 
@@ -160,7 +163,7 @@
 
     lax.fori_loop(1, LAY, cot_sends, 0)
 
-    lax.fori_loop(0, NC, own_sends, 0)
+    lax.fori_loop(FIRST, NC, own_sends, 0)
 
     pltpu.make_async_copy(q_hbm.at[d], qbuf.at[d], rcv_sem.at[2]).start()
 

time: 288 us -> 288 us (level)
  no operation moved by 1% of the time
where the time goes in v3:
time: 288 us
  Pallas kernels  284 us (99%)
  local copies, waits for them, and re-layouts  3.79 us (1%)
    pallas_call x1, Pallas kernels, local(): pl.pallas_call(functools.partial(kernel, dims), out_shape=jax.ShapeDtypeS...  284 us

profile of v3, /device:TPU:0, one launch (start us, length us, event | category | flops | bytes accessed | tf_op | source)
XLA Modules:
  0.0 288.0 jit_solution(13608455620960590144)
XLA Ops:
  0.0 0.0 copy-start
  0.0 1.0 copy-done
  1.0 0.4 bitcast_bitcast_fusion
  1.4 1.1 reshape.7.q_hbm
  2.5 284.2 %shard_map.109 = f32[8,32]{1,0:T(8,128)} custom-call(bf16[128,4096]{1,0:T(8,128)(2,1)} %act_hbm.1, bf16[512,3584]{1,0:T(8,128)(2,1)} %gate_hbm.1, bf16[512,3584]{1,0:T(8,128)(2,1)} %up_hbm.1, bf16[128,4096]{1,0:T(8,128)(2,1)} %cot_hbm.1, bf16[3584,512]{1,0:T(8,128)(2,1)} %w_hbm.1, bf16[64,4096]{1,0:T(8,128)(2,1)} %up_entry.1, bf16[64,3584]{1,0:T(8,128)(2,1)} %up_exit.1, ...), custom_call_target="tpu_custom_call" | custom-call | tf_op jit(solution)/shard_map/pallas_call | solution.py:407
  286.7 1.3 copy.16
Async XLA Ops:
  0.0 1.0 copy-start
